TPU v7x, 256 devices: a whole 4x4x8 slice. The times are simulated.
256 devices in a mesh: row: 8 (over y, core), col: 32 (over z, x).
Axes of the slice: x: 4, y: 4, z: 8, core: 2. Of those that a mesh axis runs over, the one named last changes fastest.
Arguments:
- tokens: bfloat16 [512, 12288], P('col', 'row'), may hold values from -6 to 6
- grad_out: bfloat16 [512, 12288], P('col', 'row'), may hold values from -6 to 6
- w_in: bfloat16 [12288, 24576], P('row', 'col'), may hold values from -0.0546875 to 0.0546875
- w_out: bfloat16 [24576, 12288], P('col', 'row'), may hold values from -0.0390625 to 0.0390625
Outputs:
- grad_in: bfloat16 [512, 12288], P('col', 'row')
- grad_w_in: bfloat16 [12288, 24576], P('row', 'col')
- grad_w_out: bfloat16 [24576, 12288], P('col', 'row')
All inputs are finite; a program needn't handle non-finite values.
Results may differ from a plain program's by a relative error of at most 0.022.
Values may be sent and summed in bfloat16 or wider, within the bound.
A program may use at most 64 MiB of HBM per device.

v0:
```python
import math

import jax
import jax.numpy as jnp
from jax import lax
from jax.sharding import PartitionSpec as P


def gelu_pair(pre_act, back_act):
    coeff = math.sqrt(2.0 / math.pi)
    inner = coeff * (pre_act + 0.044715 * pre_act * pre_act * pre_act)
    tanh_val = jnp.tanh(inner)
    activated = (0.5 * pre_act * (1.0 + tanh_val)).astype(jnp.bfloat16)
    slope = 0.5 * (1.0 + tanh_val) + 0.5 * pre_act * (1.0 - tanh_val * tanh_val) * coeff * (
        1.0 + 3.0 * 0.044715 * pre_act * pre_act
    )
    grad_pre = (back_act * slope).astype(jnp.bfloat16)
    return (activated, grad_pre)


def per_device(tokens, grad_out, w_in, w_out):
    all_tokens, all_grads = (
        lax.all_gather(tokens, "col", axis=0, tiled=True),
        lax.all_gather(grad_out, "col", axis=0, tiled=True),
    )
    pre_part = jnp.dot(all_tokens, w_in, preferred_element_type=jnp.float32)
    back_part = lax.dot_general(
        all_grads, w_out, (((1,), (1,)), ((), ())), preferred_element_type=jnp.float32
    )
    pre_act, back_act = lax.psum((pre_part, back_part), "row")
    activated, grad_pre = gelu_pair(pre_act, back_act)
    grad_w_out = lax.dot_general(
        activated, all_grads, (((0,), (0,)), ((), ())), preferred_element_type=jnp.float32
    ).astype(jnp.bfloat16)
    grad_w_in = lax.dot_general(
        all_tokens, grad_pre, (((0,), (0,)), ((), ())), preferred_element_type=jnp.float32
    ).astype(jnp.bfloat16)
    grad_in = lax.psum_scatter(
        lax.dot_general(
            grad_pre, w_in, (((1,), (1,)), ((), ())), preferred_element_type=jnp.float32
        ).astype(jnp.bfloat16),
        "col",
        scatter_dimension=0,
        tiled=True,
    )
    return (grad_in, grad_w_in, grad_w_out)


def solution(mesh):
    return jax.shard_map(
        per_device,
        mesh=mesh,
        in_specs=(P("col", "row"), P("col", "row"), P("row", "col"), P("col", "row")),
        out_specs=(P("col", "row"), P("row", "col"), P("col", "row")),
        check_vma=False,
    )
```

profile of v0, /device:TPU:1, one launch (start us, length us, event | category | flops | bytes accessed | tf_op | source)
XLA Modules:
  0.0 467.9 jit_solution(2856750602324072329)
XLA Ops:
  7.2 0.0 copy-start
  7.2 0.0 all-gather.3.cloned.1.call-start
  7.2 0.7 all-gather.3.cloned.1.call-update
  7.9 0.0 all-gather.5.cloned.1.call-start
  8.0 0.7 all-gather.5.cloned.1.call-update
  8.7 0.0 all-reduce.3.cloned.1.call-start
  8.7 78.6 %all-gather.3.cloned.1.call-done = bf16[512,1536]{1,0:T(8,128)(2,1)} async-done(((bf16[16,1536]{1,0:T(8,128)(2,1)}), bf16[512,1536]{1,0:T(8,128)(2,1)}) %all-gather.3.cloned.1.call-update) | async-done | bytes 1572880 | tf_op jit(solution)/shard_map/all_gather | solution.py:24
  87.3 4.7 %fusion.16 = f32[512,768]{1,0:T(8,128)} fusion(bf16[512,1536]{1,0:T(8,128)(2,1)} %all-gather.3.cloned.1.call-done, bf16[768,1536]{1,0:T(8,128)(2,1)} %param.7), kind=kOutput, calls=%fused_computation.22 | convolution fusion | flops 1207959552 | bytes 5505024 | tf_op jit(solution)/shard_map/dot_general | solution.py:27
  92.0 72.6 %all-gather.5.cloned.1.call-done = bf16[512,1536]{1,0:T(8,128)(2,1)} async-done(((bf16[16,1536]{1,0:T(8,128)(2,1)}), bf16[512,1536]{1,0:T(8,128)(2,1)}) %all-gather.5.cloned.1.call-update) | async-done | bytes 1572880 | tf_op jit(solution)/shard_map/all_gather | solution.py:23
  164.5 0.0 copy-done
  164.5 3.9 fusion.17
  168.5 0.0 all-reduce.3.cloned.1.call-update
  168.5 0.0 reduce-scatter.2.cloned.1.call-start
  168.5 74.4 %all-reduce.3.cloned.1.call-done = (f32[512,768]{1,0:T(8,128)}, f32[512,768]{1,0:T(8,128)}) async-done(((f32[512,768]{1,0:T(8,128)}, f32[512,768]{1,0:T(8,128)}), (f32[512,768]{1,0:T(8,128)}, f32[512,768]{1,0:T(8,128)})) %all-reduce.3.cloned.1.call-update) | async-done | bytes 3145744 | tf_op jit(solution)/shard_map/psum | solution.py:30
  243.0 2.9 fusion.7
  245.9 2.6 convolution_convert_fusion.2
  248.4 0.0 reduce-scatter.2.cloned.1.call-update
  248.5 4.2 fusion
  252.7 4.3 copy.7
  257.0 4.8 %convolution_convert_fusion = bf16[768,1536]{1,0:T(8,128)(2,1)} fusion(bf16[512,1536]{1,0:T(8,128)(2,1)} %all-gather.3.cloned.1.call-done, f32[512,768]{1,0:T(8,128)} %get-tuple-element.7), kind=kOutput, calls=%fused_computation | convolution fusion | flops 1212678144 | bytes 5505024 | tf_op jit(solution)/shard_map/dot_general | solution.py:32
  261.8 199.6 %reduce-scatter.2.cloned.1.call-done = bf16[16,1536]{1,0:T(8,128)(2,1)} async-done(((bf16[512,1536]{1,0:T(8,128)(2,1)}), bf16[16,1536]{1,0:T(8,128)(2,1)}) %reduce-scatter.2.cloned.1.call-update) | async-done | bytes 49168 | tf_op jit(solution)/shard_map/reduce_scatter | solution.py:38
Async XLA Ops:
  7.2 157.4 %copy-start = (bf16[1536,768]{1,0:T(8,128)(2,1)S(1)}, bf16[1536,768]{1,0:T(8,128)(2,1)}, u32[]{:S(2)}) copy-start(bf16[1536,768]{1,0:T(8,128)(2,1)} %param.6) | copy-start | bytes 7077892
  7.2 80.1 %all-gather.3.cloned.1.call-start = ((), (), s32[]{:S(2)}) async-start(), calls=%async_computation.1 | async-start | bytes 1622016 | tf_op jit(solution)/shard_map/all_gather | solution.py:24
  7.9 156.6 %all-gather.5.cloned.1.call-start = ((), (), s32[]{:S(2)}) async-start(), calls=%async_computation.2 | async-start | bytes 1622016 | tf_op jit(solution)/shard_map/all_gather | solution.py:23
  8.7 234.3 %all-reduce.3.cloned.1.call-start = ((), (), s32[]{:S(2)}) async-start(), calls=%async_computation.4 | async-start | bytes 6291456 | tf_op jit(solution)/shard_map/psum | solution.py:30
  168.5 292.9 %reduce-scatter.2.cloned.1.call-start = ((), (), s32[]{:S(2)}) async-start(), calls=%async_computation.3 | async-start | bytes 1622016 | tf_op jit(solution)/shard_map/reduce_scatter | solution.py:38
Sparse Core Ops, SparseCore 0:
  10.6 76.6 all-gather.2
  89.9 74.6 all-gather.4
  168.6 74.3 all-reduce.2
  248.6 212.7 reduce-scatter.1
where the time goes:
time: 472 us; the launch traced here: 468 us
  waiting for transfers between devices  427 us (90%)
  matrix products  20.2 us (4%)
  between operations  13.8 us (3%)
    reduce_scatter x1, waiting for transfers between devices, per_device(): lax.psum_scatter(lax.dot_general(grad_pre, w_in, (((1,), (1,)), ((), ()))...  200 us
    all_gather x1, waiting for transfers between devices, per_device(): lax.all_gather(grad_out, 'col', axis=0, tiled=True)  78.6 us
    psum x1, waiting for transfers between devices, per_device(): pre_act, back_act = lax.psum((pre_part, back_part), 'row')  74.4 us
    all_gather x1, waiting for transfers between devices, per_device(): lax.all_gather(tokens, 'col', axis=0, tiled=True)  72.6 us
  transfers between devices with their start and end apart: 4, of which 4 were waited for; matrix products, arithmetic and copies ran while one was open for 4% of the time, Pallas kernels for 0%

commit v1 on v0

v1 whole, which is shorter than its diff:
```python
import math

import jax
import jax.numpy as jnp
from jax import lax
from jax.experimental import pallas as pl
from jax.experimental.pallas import tpu as pltpu
from jax.sharding import PartitionSpec as P

F32, BF16 = jnp.float32, jnp.bfloat16
MESH = pl.DeviceIdType.MESH
D, FF, TOK = 1536, 768, 512
HALF = FF // 2
ROWS = 16
CA = 640
ZA = 256
ZB = D - ZA
GROUPS = ((0, 4), (4, 8), (12, 8), (20, 8), (28, 4))
XOFF = (0, 1, -1, 2)
ORDER = (
    ('init',), ('ax', 2), ('ax', 1), ('bz', 1, 0), ('bz', 1, 1), ('az', 1, 0, 0), ('az', 1, 1, 0), ('bx', 0, 0, 2),
    ('bx', 0, 0, 1), ('ax', 3), ('az', 1, 0, 2), ('az', 1, 1, 2), ('bx', 1, 0, 2), ('az', 1, 0, 1), ('az', 1, 1, 1),
    ('bx', 1, 0, 1), ('bx', 1, 1, 2), ('bz', 2, 0), ('bx', 1, 1, 1), ('bz', 2, 1), ('S1', 0), ('az', 1, 0, 3),
    ('az', 1, 1, 3), ('az', 2, 0, 0), ('az', 2, 1, 0), ('az', 2, 0, 2), ('az', 2, 1, 2), ('bx', 2, 0, 1),
    ('az', 2, 0, 1), ('az', 2, 1, 1), ('S2', 0), ('bx', 2, 0, 2), ('S1', 1), ('az', 2, 0, 3), ('bx', 2, 1, 1),
    ('bx', 2, 1, 2), ('az', 2, 1, 3), ('bz', 3, 0), ('bz', 3, 1), ('az', 3, 0, 0), ('az', 3, 1, 0), ('az', 3, 0, 2),
    ('az', 3, 1, 2), ('S2', 1), ('S3', 0), ('az', 3, 0, 1), ('az', 3, 1, 1), ('S1', 2), ('bx', 3, 0, 1),
    ('bx', 3, 0, 2), ('az', 3, 0, 3), ('az', 3, 1, 3), ('bz', 4, 0), ('bx', 3, 1, 1), ('bx', 3, 1, 2), ('S2', 2),
    ('S3', 1), ('S4', 0), ('bx', 4, 0, 1), ('bx', 4, 0, 2), ('S5', 0), ('S1', 3), ('S3', 2), ('S1', 4), ('S6', 0),
    ('S4', 1), ('S2', 3), ('S2', 4), ('S5', 1), ('S4', 2), ('S5', 2), ('S3', 3), ('S3', 4), ('S6', 1), ('S4', 3),
    ('S6', 2), ('S4', 4), ('S5', 3), ('S5', 4), ('W', 0), ('W', 1), ('S6', 3), ('E1',), ('S6', 4), ('E3',), ('E2',),
)


def ways(s):
    return (0, 1) if s in (1, 2, 3) else (0,)


def block(s, d, f):
    return GROUPS[s][0] + 4 * d + f


def gelu_pair(pre_act, back_act):
    coeff = math.sqrt(2.0 / math.pi)
    inner = coeff * (pre_act + 0.044715 * pre_act * pre_act * pre_act)
    tanh_val = jnp.tanh(inner)
    activated = (0.5 * pre_act * (1.0 + tanh_val)).astype(BF16)
    slope = 0.5 * (1.0 + tanh_val) + 0.5 * pre_act * (1.0 - tanh_val * tanh_val) * coeff * (
        1.0 + 3.0 * 0.044715 * pre_act * pre_act
    )
    return activated, (back_act * slope).astype(BF16)


def dot(a, b, dims):
    return lax.dot_general(a, b, ((dims[:1], dims[1:]), ((), ())), preferred_element_type=F32)


def kernel(
    tok_hbm, grad_hbm, win_hbm, wout_hbm, GIN, GW1, GW2,
    X, W1, W2, KS, KO, KR, C, R, H, G, RA, SA, RX, RB, SB, RZ, OUT,
    local_sem,
    a_send, a_recv, b_send, b_recv, k_send, k_recv, r_send, r_recv, y_send, y_recv, h_send, h_recv,
    ra_send, ra_recv, rb_send, rb_recv, rx_send, rx_recv, rz_send, rz_recv,
):
    row, col = lax.axis_index("row"), lax.axis_index("col")
    y, core, z, x = row // 2, row % 2, col // 4, col % 4

    def at(dz=0, dx=0, dy=0, other=False):
        return {
            "row": lax.rem(y + dy + 4, 4) * 2 + (1 - core if other else core),
            "col": lax.rem(z + dz + 8, 8) * 4 + lax.rem(x + dx + 4, 4),
        }

    mine = pl.multiple_of(core * HALF, HALF)
    theirs = pl.multiple_of((1 - core) * HALF, HALF)
    local = [
        pltpu.make_async_copy(tok_hbm, X.at[0, pl.ds(0, ROWS)], local_sem.at[0]),
        pltpu.make_async_copy(grad_hbm, X.at[1, pl.ds(0, ROWS)], local_sem.at[1]),
        pltpu.make_async_copy(win_hbm.at[:, pl.ds(mine, HALF)], W1.at[:, pl.ds(0, HALF)], local_sem.at[2]),
        pltpu.make_async_copy(win_hbm.at[:, pl.ds(theirs, HALF)], W1.at[:, pl.ds(HALF, HALF)], local_sem.at[3]),
        pltpu.make_async_copy(wout_hbm.at[pl.ds(mine, HALF)], W2.at[pl.ds(0, HALF)], local_sem.at[4]),
        pltpu.make_async_copy(wout_hbm.at[pl.ds(theirs, HALF)], W2.at[pl.ds(HALF, HALF)], local_sem.at[5]),
    ]
    for copy in local:
        copy.start()

    partners = [at(dz=i) for i in range(1, 8)] + [at(dx=i) for i in range(1, 4)] + [at(dy=i) for i in range(1, 4)]
    partners.append(at(other=True))
    barrier = pltpu.get_barrier_semaphore()
    for partner in partners:
        pl.semaphore_signal(barrier, inc=1, device_id=partner, device_id_type=MESH)
    pl.semaphore_wait(barrier, len(partners))

    unsent = []

    def remote(src, dst, send, recv, target):
        return pltpu.make_async_remote_copy(
            src_ref=src, dst_ref=dst, send_sem=send, recv_sem=recv, device_id=target, device_id_type=MESH
        )

    def start(copy):
        copy.start()
        unsent.append(copy)

    def piece(part, s, d, f, which):
        array = pl.ds(0, 2) if which is None else pl.ds(which, 1)
        columns = pl.ds(0, CA) if part == 0 else pl.ds(CA, D - CA)
        return X.at[array, pl.ds(ROWS * block(s, d, f), ROWS), columns]

    def gather(part, src, dst, target, which=None):
        i = 2 * block(*dst) + (which or 0)
        send, recv = (a_send, a_recv) if part == 0 else (b_send, b_recv)
        return remote(piece(part, *src, which), piece(part, *dst, which), send.at[i], recv.at[i], target)

    def arrived(part, s, d, f, which=None):
        gather(part, (s, d, f), (s, d, f), at(dz=1), which).wait_recv()

    def along_z(part, s, d, f):
        if s == 0:
            start(gather(part, (0, 0, f), (1, 0, f), at(dz=1)))
            start(gather(part, (0, 0, f), (1, 1, f), at(dz=-1)))
        elif s < 3:
            start(gather(part, (s, d, f), (s + 1, d, f), at(dz=-1 if d else 1)))
        elif s == 3:
            start(gather(part, (3, d, f), (4, 0, f), at(dz=-1 if d else 1), d))

    def along_x(part, s, d):
        start(gather(part, (s, d, 0), (s, d, 2), at(dx=1)))
        start(gather(part, (s, d, 0), (s, d, 1), at(dx=-1)))

    def further_x(part, s, d, f):
        start(gather(part, (s, d, f), (s, d, 3), at(dx=-1 if f == 1 else 1), f - 1))

    def begin():
        local[0].wait()
        local[1].wait()
        along_z(1, 0, 0, 0)
        along_x(0, 0, 0)
        along_z(0, 0, 0, 0)
        along_x(1, 0, 0)

    def ax(f):
        if f == 3:
            arrived(0, 0, 0, 3, 0)
            arrived(0, 0, 0, 3, 1)
        else:
            arrived(0, 0, 0, f)
        along_z(0, 0, 0, f)
        if f < 3:
            further_x(0, 0, 0, f)

    def az(s, d, f):
        arrived(0, s, d, f)
        along_z(0, s, d, f)

    def bz(s, d):
        if s == 4:
            arrived(1, 4, 0, 0, 0)
            arrived(1, 4, 0, 0, 1)
        else:
            arrived(1, s, d, 0)
        along_z(1, s, d, 0)
        along_x(1, s, d)

    def bx(s, d, f):
        arrived(1, s, d, f)
        further_x(1, s, d, f)

    def rows(s):
        return ROWS * GROUPS[s][0], ROWS * GROUPS[s][1]

    def swap_copy(s):
        first, n = rows(s)
        part = pl.ds(first, n)
        return remote(KS.at[:, part], KR.at[:, part], k_send.at[s], k_recv.at[s], at(other=True))

    def s1(s):
        for d in ways(s):
            arrived(1, s, d, 3, 0)
            arrived(1, s, d, 3, 1)
        if s == 4:
            for f in range(4):
                arrived(0, 4, 0, f, 0)
                arrived(0, 4, 0, f, 1)
        first, n = rows(s)
        part = pl.ds(first, n)
        if s == 0:
            local[2].wait()
            local[3].wait()
        pre = dot(X[0, part, :], W1[...], (1, 0))
        KO[0, part, :] = pre[:, :HALF]
        KS[0, part, :] = pre[:, HALF:].astype(BF16)
        if s == 0:
            local[4].wait()
            local[5].wait()
        back = dot(X[1, part, :], W2[...], (1, 1))
        KO[1, part, :] = back[:, :HALF]
        KS[1, part, :] = back[:, HALF:].astype(BF16)
        start(swap_copy(s))

    def quarter(s, i):
        first, n = rows(s)
        return pl.ds(pl.multiple_of(first + i * (n // 4), ROWS), n // 4)

    def sum_copy(s, dy):
        n = rows(s)[1] // 4
        there = R.at[dy - 1, :, pl.ds(rows(s)[0] // 4, n)]
        return remote(
            C.at[:, quarter(s, lax.rem(y + dy, 4))], there, r_send.at[s, dy - 1], r_recv.at[s, dy - 1], at(dy=dy)
        )

    def s2(s):
        first, n = rows(s)
        part = pl.ds(first, n)
        swap_copy(s).wait_recv()
        C[:, part, :] = (KO[:, part, :] + KR[:, part, :].astype(F32)).astype(BF16)
        for dy in (2, 1, 3):
            start(sum_copy(s, dy))

    def part_copy(s, dy):
        where = H.at[:, quarter(s, y), pl.ds(0, HALF)]
        return remote(where, where, y_send.at[s, dy - 1], y_recv.at[s, dy - 1], at(dy=dy))

    def s3(s):
        for dy in (1, 2, 3):
            sum_copy(s, dy).wait_recv()
        total = C[:, quarter(s, y), :].astype(F32)
        for i in range(3):
            total += R[i, :, pl.ds(rows(s)[0] // 4, rows(s)[1] // 4), :].astype(F32)
        activated, grad_pre = gelu_pair(total[0], total[1])
        H[0, quarter(s, y), 0:HALF] = activated
        H[1, quarter(s, y), 0:HALF] = grad_pre
        for dy in (2, 1, 3):
            start(part_copy(s, dy))

    def half_copy(s):
        first, n = rows(s)
        part = pl.ds(first, n)
        return remote(
            H.at[:, part, pl.ds(0, HALF)], H.at[:, part, pl.ds(HALF, HALF)], h_send.at[s], h_recv.at[s], at(other=True)
        )

    def s4(s):
        for dy in (1, 2, 3):
            part_copy(s, dy).wait_recv()
        start(half_copy(s))

    def ra_copy(s, d):
        i = 2 * (s - 1) + d
        there = RA.at[i]
        src = G.at[pl.ds(ROWS * block(s, d, 0), 4 * ROWS), pl.ds(0, ZA)]
        return remote(src, there, ra_send.at[i], ra_recv.at[i], at(dz=s if d else -s))

    def rb_copy(s, d, f):
        i, j = 2 * s + d, f - 1
        src = G.at[pl.ds(ROWS * block(s, d, f), ROWS), pl.ds(ZA, ZB)]
        return remote(src, RB.at[i, j], rb_send.at[i, j], rb_recv.at[i, j], at(dx=XOFF[f]))

    def rz_copy(s, d):
        i = 2 * (s - 1) + d
        return remote(SB.at[i], RZ.at[i], rz_send.at[i], rz_recv.at[i], at(dz=s if d else -s))

    def rx_copy(f):
        src = SA.at[pl.ds(ROWS * f, ROWS)]
        return remote(src, RX.at[f - 1], rx_send.at[f - 1], rx_recv.at[f - 1], at(dx=XOFF[f]))

    def s5(s):
        half_copy(s).wait_recv()
        first, n = rows(s)
        part = pl.ds(first, n)
        G[part, :] = dot(H[1, part, :], W1[...], (1, 1)).astype(BF16)
        for d in ways(s):
            if s:
                start(ra_copy(s, d))
            for f in (3, 1, 2):
                start(rb_copy(s, d, f))

    def s6(s):
        for d in ways(s):
            for f in (1, 2, 3):
                rb_copy(s, d, f).wait_recv()
            i = 2 * s + d
            total = G[pl.ds(ROWS * block(s, d, 0), ROWS), pl.ds(ZA, ZB)].astype(F32)
            for j in range(3):
                total += RB[i, j].astype(F32)
            if s:
                SB[2 * (s - 1) + d] = total.astype(BF16)
                start(rz_copy(s, d))
            else:
                OUT[:, pl.ds(ZA, ZB)] = total

    def w(i):
        if i == 0:
            total = dot(X[0], H[1], (0, 0)).astype(BF16)
            GW1[:, pl.ds(mine, HALF)] = total[:, :HALF]
            GW1[:, pl.ds(theirs, HALF)] = total[:, HALF:]
        else:
            total = dot(H[0], X[1], (0, 0)).astype(BF16)
            GW2[pl.ds(mine, HALF), :] = total[:HALF]
            GW2[pl.ds(theirs, HALF), :] = total[HALF:]

    def e1():
        for s in (1, 2, 3, 4):
            for d in ways(s):
                ra_copy(s, d).wait_recv()
        total = G[pl.ds(0, 4 * ROWS), pl.ds(0, ZA)].astype(F32)
        for i in range(7):
            total += RA[i].astype(F32)
        OUT[:, pl.ds(0, ZA)] = total[:ROWS]
        SA[...] = total.astype(BF16)
        for f in (3, 1, 2):
            start(rx_copy(f))

    def e2():
        for s in (1, 2, 3, 4):
            for d in ways(s):
                rz_copy(s, d).wait_recv()
        total = OUT[:, pl.ds(ZA, ZB)]
        for i in range(7):
            total += RZ[i].astype(F32)
        GIN[:, pl.ds(ZA, ZB)] = total.astype(BF16)

    def e3():
        for f in (1, 2, 3):
            rx_copy(f).wait_recv()
        total = OUT[:, pl.ds(0, ZA)]
        for i in range(3):
            total += RX[i].astype(F32)
        GIN[:, pl.ds(0, ZA)] = total.astype(BF16)

    def drain():
        for copy in unsent:
            copy.wait_send()
        unsent.clear()

    steps = {
        "init": begin, "ax": ax, "az": az, "bz": bz, "bx": bx, "S1": s1, "S2": s2, "S3": s3, "S4": s4, "S5": s5, "S6": s6,
        "W": w, "E1": e1, "E2": e2, "E3": e3, "drain": drain,
    }
    for name, *args in ORDER:
        steps[name](*args)
    drain()


def write_out(a, b, c, a_hbm, b_hbm, c_hbm, sem):
    copies = [pltpu.make_async_copy(a, a_hbm, sem.at[0])]
    for i, (src, dst) in enumerate(((b, b_hbm), (c, c_hbm))):
        n = src.shape[0] // 2
        for j in range(2):
            part = pl.ds(j * n, n)
            copies.append(pltpu.make_async_copy(src.at[part], dst.at[part], sem.at[1 + 2 * i + j]))
    for copy in copies:
        copy.start()
    for copy in copies:
        copy.wait()


def per_device(tokens, grad_out, w_in, w_out):
    hbm, vmem = pl.BlockSpec(memory_space=pltpu.HBM), pl.BlockSpec(memory_space=pltpu.VMEM)
    dma = pltpu.SemaphoreType.DMA
    scratch = [
        pltpu.VMEM((2, TOK, D), BF16),
        pltpu.VMEM((D, FF), BF16),
        pltpu.VMEM((FF, D), BF16),
        pltpu.VMEM((2, TOK, HALF), BF16),
        pltpu.VMEM((2, TOK, HALF), F32),
        pltpu.VMEM((2, TOK, HALF), BF16),
        pltpu.VMEM((2, TOK, HALF), BF16),
        pltpu.VMEM((3, 2, TOK // 4, HALF), BF16),
        pltpu.VMEM((2, TOK, FF), BF16),
        pltpu.VMEM((TOK, D), BF16),
        pltpu.VMEM((7, 4 * ROWS, ZA), BF16),
        pltpu.VMEM((4 * ROWS, ZA), BF16),
        pltpu.VMEM((3, ROWS, ZA), BF16),
        pltpu.VMEM((9, 3, ROWS, ZB), BF16),
        pltpu.VMEM((7, ROWS, ZB), BF16),
        pltpu.VMEM((7, ROWS, ZB), BF16),
        pltpu.VMEM((ROWS, D), F32),
        dma((6,)),
    ]
    for shape in ((64,), (64,), (5,), (5, 3), (5, 3), (5,), (7,), (9, 3), (3,), (7,)):
        scratch += [dma(shape), dma(shape)]
    results = (
        jax.ShapeDtypeStruct((ROWS, D), BF16),
        jax.ShapeDtypeStruct((D, FF), BF16),
        jax.ShapeDtypeStruct((FF, D), BF16),
    )
    held = pl.pallas_call(
        kernel,
        out_shape=tuple(pltpu.VMEM(r.shape, r.dtype) for r in results),
        in_specs=[hbm] * 4,
        out_specs=(vmem, vmem, vmem),
        scratch_shapes=scratch,
        compiler_params=pltpu.CompilerParams(collective_id=0, has_side_effects=True, vmem_limit_bytes=40 * 2**20),
        cost_estimate=pl.CostEstimate(flops=10 * TOK * D * FF, bytes_accessed=8 * D * FF, transcendentals=TOK * HALF // 4),
    )(*(pltpu.with_memory_space_constraint(arg, pltpu.HBM) for arg in (tokens, grad_out, w_in, w_out)))
    return pl.pallas_call(
        write_out,
        out_shape=tuple(pltpu.HBM(r.shape, r.dtype) for r in results),
        in_specs=[vmem] * 3,
        out_specs=(hbm, hbm, hbm),
        scratch_shapes=[dma((5,))],
        cost_estimate=pl.CostEstimate(flops=0, bytes_accessed=8 * D * FF, transcendentals=0),
    )(*held)


def solution(mesh):
    return jax.shard_map(
        per_device,
        mesh=mesh,
        in_specs=(P("col", "row"), P("col", "row"), P("row", "col"), P("col", "row")),
        out_specs=(P("col", "row"), P("row", "col"), P("col", "row")),
        check_vma=False,
    )
```

time: 472 us -> 78.1 us (0.17)
  waiting for transfers between devices: 427 us -> 0 us
  Pallas kernels: 0 us -> 73.9 us
  matrix products: 20.2 us -> 0 us
  between operations: 13.8 us -> 0.65 us
    reduce_scatter x1 -> x0, waiting for transfers between devices: 200 us -> none  [per_device(): lax.psum_scatter(lax.dot_general(grad_pre, w_in, (((1,), (1,)), ((), ()))...]
    all_gather x2 -> x0, waiting for transfers between devices: 151 us -> none  [the longest x1 78.6 us: per_device(): lax.all_gather(grad_out, 'col', axis=0, tiled=True)]
    psum x1 -> x0, waiting for transfers between devices: 74.4 us -> none  [per_device(): pre_act, back_act = lax.psum((pre_part, back_part), 'row')]
    pallas_call x0 -> x2, Pallas kernels: none -> 73.9 us  [the longest x1 69.3 us: per_device(): pl.pallas_call(kernel, out_shape=tuple((pltpu.VMEM(r.shape, r.dtype) for...]
    dot_general x5 -> x0, matrix products: 20.2 us -> none  [the longest x1 4.79 us: per_device(): lax.dot_general(activated, all_grads, (((0,), (0,)), ((), ())), preferred...]
  transfers between devices with their start and end apart: 4 -> 0, of which waited for: 4 -> 0; matrix products, arithmetic and copies ran while one was open for 4% -> 0% of each run, Pallas kernels for 0% -> 0%
where the time goes in v1:
time: 78.1 us; the launch traced here: 78 us
  Pallas kernels  73.9 us (95%)
  local copies, waits for them, and re-layouts  3.43 us (4%)
    pallas_call x1, Pallas kernels, per_device(): pl.pallas_call(kernel, out_shape=tuple((pltpu.VMEM(r.shape, r.dtype) for...  69.3 us
    pallas_call x1, Pallas kernels, per_device(): pl.pallas_call(write_out, out_shape=tuple((pltpu.HBM(r.shape, r.dtype) fo...  4.63 us
    unnamed x6, local copies, waits for them, and re-layouts  3.43 us

profile of v1, /device:TPU:1, one launch (start us, length us, event | category | flops | bytes accessed | tf_op | source)
XLA Modules:
  0.0 78.0 jit_solution(11615094687105328228)
XLA Ops:
  0.6 69.3 %shard_map.67 = (bf16[16,1536]{1,0:T(8,128)(2,1)S(1)}, bf16[1536,768]{1,0:T(8,128)(2,1)S(1)}, bf16[768,1536]{1,0:T(8,128)(2,1)S(1)}) custom-call(bf16[16,1536]{1,0:T(8,128)(2,1)} %tok_hbm.1, bf16[16,1536]{1,0:T(8,128)(2,1)} %grad_hbm.1, bf16[1536,768]{1,0:T(8,128)(2,1)} %win_hbm.1, bf16[768,1536]{1,0:T(8,128)(2,1)} %wout_hbm.1), custom_call_target="tpu_custom_call" | custom-call | flops 6039797760 | bytes 9437184 | tf_op jit(solution)/shard_map/pallas_call | solution.py:388
  69.9 0.0 copy-start
  69.9 1.4 %copy-done = bf16[1536,768]{1,0:T(8,128)(2,1)} copy-done((bf16[1536,768]{1,0:T(8,128)(2,1)}, bf16[1536,768]{1,0:T(8,128)(2,1)S(1)}, u32[]{:S(2)}) %copy-start) | copy-done | bytes 2359320
  71.3 0.0 copy-start.1
  71.3 1.4 %copy-done.1 = bf16[768,1536]{1,0:T(8,128)(2,1)} copy-done((bf16[768,1536]{1,0:T(8,128)(2,1)}, bf16[768,1536]{1,0:T(8,128)(2,1)S(1)}, u32[]{:S(2)}) %copy-start.1) | copy-done | bytes 2359320
  72.7 0.0 copy-start.2
  72.7 0.6 copy-done.2
  73.4 4.6 %shard_map.68 = (bf16[16,1536]{1,0:T(8,128)(2,1)}, bf16[1536,768]{1,0:T(8,128)(2,1)}, bf16[768,1536]{1,0:T(8,128)(2,1)}) custom-call(bf16[16,1536]{1,0:T(8,128)(2,1)} %copy-done.2, bf16[1536,768]{1,0:T(8,128)(2,1)} %copy-done, bf16[768,1536]{1,0:T(8,128)(2,1)} %copy-done.1), custom_call_target="tpu_custom_call" | custom-call | bytes 9437184 | tf_op jit(solution)/shard_map/pallas_call | solution.py:397
Async XLA Ops:
  69.9 1.4 %copy-start = (bf16[1536,768]{1,0:T(8,128)(2,1)}, bf16[1536,768]{1,0:T(8,128)(2,1)S(1)}, u32[]{:S(2)}) copy-start(bf16[1536,768]{1,0:T(8,128)(2,1)S(1)} %get-tuple-element.7.b) | copy-start | bytes 7077892
  71.3 1.4 %copy-start.1 = (bf16[768,1536]{1,0:T(8,128)(2,1)}, bf16[768,1536]{1,0:T(8,128)(2,1)S(1)}, u32[]{:S(2)}) copy-start(bf16[768,1536]{1,0:T(8,128)(2,1)S(1)} %get-tuple-element.8.c) | copy-start | bytes 7077892
  72.7 0.6 copy-start.2

commit v2 on v1

v2 whole, which is shorter than its diff:
```python
import math

import jax
import jax.numpy as jnp
from jax import lax
from jax.experimental import pallas as pl
from jax.experimental.pallas import tpu as pltpu
from jax.sharding import PartitionSpec as P

F32, BF16 = jnp.float32, jnp.bfloat16
MESH = pl.DeviceIdType.MESH
D, FF, TOK = 1536, 768, 512
HALF = FF // 2
ROWS = 16
DIRECT = (4,)
CA = 640
ZA = 384
ZB = D - ZA
GROUPS = ((0, 4), (4, 8), (12, 8), (20, 8), (28, 4))
XOFF = (0, 1, -1, 2)
ORDER = (
    ("z", 1, 0, 0, 0), ("x", 0, 0, 0), ("T", 2, 0), ("T", 2, 1), ("z", 0, 0, 0, 0), ("T", 2, 2), ("x", 1, 0, 0),
    ("f", 0, 0, 0, 1), ("f", 0, 0, 0, 2), ("z", 1, 1, 1, 0), ("x", 1, 1, 0), ("z", 1, 1, 0, 0), ("x", 1, 1, 1),
    ("z", 0, 0, 0, 2), ("T", 1, 1), ("z", 0, 0, 0, 3), ("f", 1, 0, 0, 2), ("z", 0, 0, 0, 1), ("f", 1, 0, 0, 1),
    ("x", 1, 2, 1), ("x", 1, 2, 0), ("z", 1, 2, 0, 0), ("z", 0, 1, 1, 0), ("z", 0, 1, 0, 0), ("f", 1, 1, 1, 1),
    ("z", 1, 2, 1, 0), ("z", 0, 1, 0, 3), ("f", 1, 1, 0, 1), ("f", 1, 1, 0, 2), ("T", 1, 0), ("z", 0, 1, 1, 2),
    ("f", 1, 1, 1, 2), ("P", 0), ("z", 0, 1, 0, 1), ("f", 1, 2, 1, 1), ("f", 1, 2, 1, 2), ("Q", 0), ("x", 1, 3, 0),
    ("z", 0, 1, 0, 2), ("z", 0, 1, 1, 1), ("z", 1, 3, 0, 0), ("f", 1, 2, 0, 1), ("f", 1, 2, 0, 2), ("x", 1, 3, 1),
    ("z", 1, 3, 1, 0), ("z", 0, 1, 1, 3), ("z", 0, 2, 1, 0), ("z", 0, 2, 0, 0), ("T", 1, 5), ("S2", 0),
    ("z", 0, 2, 0, 3), ("P", 1), ("Q", 1), ("f", 1, 3, 0, 1), ("f", 1, 3, 0, 2), ("z", 0, 2, 1, 2), ("z", 0, 2, 0, 1),
    ("z", 0, 2, 0, 2), ("S2", 1), ("z", 0, 2, 1, 1), ("P", 2), ("z", 0, 2, 1, 3), ("f", 1, 3, 1, 2), ("f", 1, 3, 1, 1),
    ("Q", 2), ("z", 0, 3, 1, 0), ("S2", 2), ("z", 0, 3, 0, 0), ("x", 1, 4, 0), ("P", 3), ("z", 0, 3, 1, 1),
    ("z", 0, 3, 0, 2), ("S3", 1), ("Q", 3), ("z", 0, 3, 0, 1), ("z", 0, 3, 1, 2), ("z", 0, 3, 1, 3), ("z", 0, 3, 0, 3),
    ("T", 1, 2), ("S2", 3), ("T", 1, 4), ("S3", 2), ("P", 4), ("Q", 4), ("S4", 1), ("S2", 4), ("T", 1, 3), ("S3", 3),
    ("S5", 1), ("S3", 0), ("S4", 2), ("S3", 4), ("S5", 2), ("S4", 3), ("S6", 1, 1), ("S4", 0), ("S6", 1, 0), ("S5", 3),
    ("S4", 4), ("S5", 4), ("S5", 0), ("S6", 2, 1), ("S6", 2, 0), ("S6", 4, 0), ("S6", 3, 0), ("S6", 3, 1), ("W", 0),
    ("E1",), ("S6", 0, 0), ("W", 1), ("E3",), ("E2",),
)


def ways(s):
    return (0, 1) if s in (1, 2, 3) else (0,)


def block(s, d, f):
    return GROUPS[s][0] + 4 * d + f


def gelu_pair(pre_act, back_act):
    coeff = math.sqrt(2.0 / math.pi)
    inner = coeff * (pre_act + 0.044715 * pre_act * pre_act * pre_act)
    tanh_val = jnp.tanh(inner)
    activated = (0.5 * pre_act * (1.0 + tanh_val)).astype(BF16)
    slope = 0.5 * (1.0 + tanh_val) + 0.5 * pre_act * (1.0 - tanh_val * tanh_val) * coeff * (
        1.0 + 3.0 * 0.044715 * pre_act * pre_act
    )
    return activated, (back_act * slope).astype(BF16)


def dot(a, b, dims):
    return lax.dot_general(a, b, ((dims[:1], dims[1:]), ((), ())), preferred_element_type=F32)


def kernel(
    tok_hbm, grad_hbm, win_hbm, wout_hbm, GIN, GW1, GW2,
    X, W1, W2, W1T, W2T, KS, KO, KR, C, R, H, G, RA, SA, RX, RB, SB, RZ, OUT,
    local_sem, sent,
    a_recv, b_recv, k_recv, r_recv, y_recv, h_recv, ra_recv, rb_recv, rx_recv, rz_recv,
):
    row, col = lax.axis_index("row"), lax.axis_index("col")
    y, core, z, x = row // 2, row % 2, col // 4, col % 4

    def at(dz=0, dx=0, dy=0, other=False):
        return {
            "row": lax.rem(y + dy + 4, 4) * 2 + (1 - core if other else core),
            "col": lax.rem(z + dz + 8, 8) * 4 + lax.rem(x + dx + 4, 4),
        }

    mine = pl.multiple_of(core * HALF, HALF)
    theirs = pl.multiple_of((1 - core) * HALF, HALF)
    local = [
        pltpu.make_async_copy(tok_hbm, X.at[0, pl.ds(0, ROWS)], local_sem.at[0]),
        pltpu.make_async_copy(grad_hbm, X.at[1, pl.ds(0, ROWS)], local_sem.at[1]),
        pltpu.make_async_copy(win_hbm.at[:, pl.ds(mine, HALF)], W1.at[:, pl.ds(0, HALF)], local_sem.at[2]),
        pltpu.make_async_copy(win_hbm.at[:, pl.ds(theirs, HALF)], W1.at[:, pl.ds(HALF, HALF)], local_sem.at[3]),
        pltpu.make_async_copy(wout_hbm.at[pl.ds(mine, HALF)], W2.at[pl.ds(0, HALF)], local_sem.at[4]),
        pltpu.make_async_copy(wout_hbm.at[pl.ds(theirs, HALF)], W2.at[pl.ds(HALF, HALF)], local_sem.at[5]),
    ]
    for copy in local:
        copy.start()

    partners = [at(dz=i) for i in range(1, 8)] + [at(dx=i) for i in range(1, 4)] + [at(dy=i) for i in range(1, 4)]
    partners.append(at(other=True))
    barrier = pltpu.get_barrier_semaphore()
    for partner in partners:
        pl.semaphore_signal(barrier, inc=1, device_id=partner, device_id_type=MESH)
    pl.semaphore_wait(barrier, len(partners))

    done = set()

    def once(key):
        new = key not in done
        done.add(key)
        return new

    def remote(src, dst, kind, recv, target):
        return pltpu.make_async_remote_copy(
            src_ref=src, dst_ref=dst, send_sem=sent.at[kind], recv_sem=recv, device_id=target, device_id_type=MESH
        )

    def piece(part, s, d, f, which):
        array = pl.ds(0, 2) if which is None else pl.ds(which, 1)
        columns = pl.ds(0, CA) if part == 0 else pl.ds(CA, D - CA)
        return X.at[array, pl.ds(ROWS * block(s, d, f), ROWS), columns]

    def gather(part, src, dst, target, which=None):
        recv = (a_recv, b_recv)[part].at[block(*dst)]
        return remote(piece(part, *src, which), piece(part, *dst, which), part, recv, target)

    def arrived(part, s, d, f):
        if s == f == 0:
            if once("own"):
                local[0].wait()
                local[1].wait()
        elif once((part, s, d, f)):
            gather(part, (s, d, f), (s, d, f), at(dz=1)).wait_recv()

    def along_z(part, s, d, f):
        arrived(part, s, d, f)
        if s == 0:
            gather(part, (0, 0, f), (1, 0, f), at(dz=1)).start()
            gather(part, (0, 0, f), (1, 1, f), at(dz=-1)).start()
        elif s < 3:
            gather(part, (s, d, f), (s + 1, d, f), at(dz=-1 if d else 1)).start()
        else:
            gather(part, (3, d, f), (4, 0, f), at(dz=-1 if d else 1), d).start()

    def along_x(part, s, d):
        arrived(part, s, d, 0)
        gather(part, (s, d, 0), (s, d, 2), at(dx=1)).start()
        gather(part, (s, d, 0), (s, d, 1), at(dx=-1)).start()
        if part == 1 and s in DIRECT:
            gather(part, (s, d, 0), (s, d, 3), at(dx=2)).start()

    def further_x(part, s, d, f):
        arrived(part, s, d, f)
        gather(part, (s, d, f), (s, d, 3), at(dx=-1 if f == 1 else 1), f - 1).start()

    def weights(i):
        if once(("weights", i)):
            local[2 * i].wait()
            local[2 * i + 1].wait()

    def turn(i, j):
        weights(i)
        part = pl.ds(256 * j, 256)
        if i == 1:
            W1T[:, part] = W1[part, :].T
        else:
            W2T[:, part] = W2[part, :].T

    def rows(s):
        return ROWS * GROUPS[s][0], ROWS * GROUPS[s][1]

    def swap_copy(s, i):
        first, n = rows(s)
        part = pl.ds(first, n)
        return remote(KS.at[i, part], KR.at[i, part], 2, k_recv.at[s, i], at(other=True))

    def product(s, i):
        first, n = rows(s)
        part = pl.ds(first, n)
        total = dot(X[i, part, :], (W1, W2T)[i][...], (1, 0))
        KO[i, part, :] = total[:, :HALF]
        KS[i, part, :] = total[:, HALF:].astype(BF16)
        swap_copy(s, i).start()

    def p(s):
        for d in ways(s):
            for f in range(4):
                arrived(0, s, d, f)
                arrived(1, s, d, f)
        weights(1)
        product(s, 0)

    def q(s):
        product(s, 1)

    def quarter(s, i):
        first, n = rows(s)
        return pl.ds(pl.multiple_of(first + i * (n // 4), ROWS), n // 4)

    def sum_copy(s, dy):
        n = rows(s)[1] // 4
        there = R.at[dy - 1, :, pl.ds(rows(s)[0] // 4, n)]
        return remote(C.at[:, quarter(s, lax.rem(y + dy, 4))], there, 3, r_recv.at[s], at(dy=dy))

    def s2(s):
        first, n = rows(s)
        part = pl.ds(first, n)
        swap_copy(s, 0).wait_recv()
        swap_copy(s, 1).wait_recv()
        C[:, part, :] = (KO[:, part, :] + KR[:, part, :].astype(F32)).astype(BF16)
        for dy in (2, 1, 3):
            sum_copy(s, dy).start()

    def part_copy(s, dy):
        where = H.at[:, quarter(s, y), pl.ds(0, HALF)]
        return remote(where, where, 4, y_recv.at[s], at(dy=dy))

    def s3(s):
        part = pl.ds(rows(s)[0] // 4, rows(s)[1] // 4)
        landed = R.at[:, :, part]
        remote(landed, landed, 3, r_recv.at[s], at(dy=1)).wait_recv()
        total = C[:, quarter(s, y), :].astype(F32)
        for i in range(3):
            total += R[i, :, part, :].astype(F32)
        activated, grad_pre = gelu_pair(total[0], total[1])
        H[0, quarter(s, y), 0:HALF] = activated
        H[1, quarter(s, y), 0:HALF] = grad_pre
        for dy in (2, 1, 3):
            part_copy(s, dy).start()

    def half_copy(s):
        first, n = rows(s)
        part = pl.ds(first, n)
        return remote(H.at[:, part, pl.ds(0, HALF)], H.at[:, part, pl.ds(HALF, HALF)], 5, h_recv.at[s], at(other=True))

    def s4(s):
        first, n = rows(s)
        landed = H.at[:, pl.ds(first, 3 * n // 4), pl.ds(0, HALF)]
        remote(landed, landed, 4, y_recv.at[s], at(dy=1)).wait_recv()
        half_copy(s).start()

    def ra_copy(s, d):
        i = 2 * (s - 1) + d
        src = G.at[pl.ds(ROWS * block(s, d, 0), 4 * ROWS), pl.ds(0, ZA)]
        return remote(src, RA.at[i], 6, ra_recv, at(dz=s if d else -s))

    def rb_copy(s, d, f):
        i = 2 * s + d
        src = G.at[pl.ds(ROWS * block(s, d, f), ROWS), pl.ds(ZA, ZB)]
        return remote(src, RB.at[i, f - 1], 7, rb_recv.at[i], at(dx=XOFF[f]))

    def rz_copy(s, d):
        i = 2 * (s - 1) + d
        return remote(SB.at[i], RZ.at[i], 8, rz_recv, at(dz=s if d else -s))

    def rx_copy(f):
        src = SA.at[pl.ds(ROWS * f, ROWS)]
        return remote(src, RX.at[f - 1], 9, rx_recv, at(dx=XOFF[f]))

    def s5(s):
        half_copy(s).wait_recv()
        first, n = rows(s)
        part = pl.ds(first, n)
        G[part, :] = dot(H[1, part, :], W1T[...], (1, 0)).astype(BF16)
        for d in ways(s):
            for f in (3, 1, 2):
                rb_copy(s, d, f).start()
            if s:
                ra_copy(s, d).start()

    def s6(s, d):
        i = 2 * s + d
        remote(RB.at[i], RB.at[i], 7, rb_recv.at[i], at(dx=1)).wait_recv()
        total = G[pl.ds(ROWS * block(s, d, 0), ROWS), pl.ds(ZA, ZB)].astype(F32)
        for j in range(3):
            total += RB[i, j].astype(F32)
        if s:
            SB[2 * (s - 1) + d] = total.astype(BF16)
            rz_copy(s, d).start()
        else:
            OUT[:, pl.ds(ZA, ZB)] = total

    def w(i):
        if i == 0:
            total = dot(X[0], H[1], (0, 0)).astype(BF16)
            GW1[:, pl.ds(mine, HALF)] = total[:, :HALF]
            GW1[:, pl.ds(theirs, HALF)] = total[:, HALF:]
        else:
            total = dot(H[0], X[1], (0, 0)).astype(BF16)
            GW2[pl.ds(mine, HALF), :] = total[:HALF]
            GW2[pl.ds(theirs, HALF), :] = total[HALF:]

    def e1():
        remote(RA, RA, 6, ra_recv, at(dz=1)).wait_recv()
        total = G[pl.ds(0, 4 * ROWS), pl.ds(0, ZA)].astype(F32)
        for i in range(7):
            total += RA[i].astype(F32)
        OUT[:, pl.ds(0, ZA)] = total[:ROWS]
        SA[...] = total.astype(BF16)
        for f in (3, 1, 2):
            rx_copy(f).start()

    def e2():
        remote(RZ, RZ, 8, rz_recv, at(dz=1)).wait_recv()
        total = OUT[:, pl.ds(ZA, ZB)]
        for i in range(7):
            total += RZ[i].astype(F32)
        GIN[:, pl.ds(ZA, ZB)] = total.astype(BF16)

    def e3():
        remote(RX, RX, 9, rx_recv, at(dx=1)).wait_recv()
        total = OUT[:, pl.ds(0, ZA)]
        for i in range(3):
            total += RX[i].astype(F32)
        GIN[:, pl.ds(0, ZA)] = total.astype(BF16)

    steps = {
        "z": along_z, "x": along_x, "f": further_x, "T": turn, "P": p, "Q": q, "S2": s2, "S3": s3, "S4": s4, "S5": s5,
        "S6": s6, "W": w, "E1": e1, "E2": e2, "E3": e3,
    }
    for name, *args in ORDER:
        steps[name](*args)
    moved = 31 * ROWS
    for kind, ref in enumerate((
        X.at[:, pl.ds(0, moved), pl.ds(0, CA)],
        X.at[:, pl.ds(0, moved), pl.ds(CA, D - CA)],
        KS,
        C.at[:, pl.ds(0, 3 * TOK // 4)],
        H.at[:, pl.ds(0, 3 * TOK // 4), pl.ds(0, HALF)],
        H.at[:, :, pl.ds(0, HALF)],
        RA,
        G.at[pl.ds(0, 24 * ROWS), pl.ds(ZA, ZB)],
        SB,
        RX,
    )):
        remote(ref, ref, kind, rx_recv, at(dz=1)).wait_send()


def write_out(a, b, c, a_hbm, b_hbm, c_hbm, sem):
    copies = [pltpu.make_async_copy(a, a_hbm, sem.at[0])]
    for i, (src, dst) in enumerate(((b, b_hbm), (c, c_hbm))):
        n = src.shape[0] // 2
        for j in range(2):
            part = pl.ds(j * n, n)
            copies.append(pltpu.make_async_copy(src.at[part], dst.at[part], sem.at[1 + 2 * i + j]))
    for copy in copies:
        copy.start()
    for copy in copies:
        copy.wait()


def per_device(tokens, grad_out, w_in, w_out):
    hbm, vmem = pl.BlockSpec(memory_space=pltpu.HBM), pl.BlockSpec(memory_space=pltpu.VMEM)
    dma = pltpu.SemaphoreType.DMA
    scratch = [
        pltpu.VMEM((2, TOK, D), BF16),
        pltpu.VMEM((D, FF), BF16),
        pltpu.VMEM((FF, D), BF16),
        pltpu.VMEM((FF, D), BF16),
        pltpu.VMEM((D, FF), BF16),
        pltpu.VMEM((2, TOK, HALF), BF16),
        pltpu.VMEM((2, TOK, HALF), F32),
        pltpu.VMEM((2, TOK, HALF), BF16),
        pltpu.VMEM((2, TOK, HALF), BF16),
        pltpu.VMEM((3, 2, TOK // 4, HALF), BF16),
        pltpu.VMEM((2, TOK, FF), BF16),
        pltpu.VMEM((TOK, D), BF16),
        pltpu.VMEM((7, 4 * ROWS, ZA), BF16),
        pltpu.VMEM((4 * ROWS, ZA), BF16),
        pltpu.VMEM((3, ROWS, ZA), BF16),
        pltpu.VMEM((9, 3, ROWS, ZB), BF16),
        pltpu.VMEM((7, ROWS, ZB), BF16),
        pltpu.VMEM((7, ROWS, ZB), BF16),
        pltpu.VMEM((ROWS, D), F32),
        dma((6,)),
        dma((10,)),
    ]
    for shape in ((32,), (32,), (5, 2), (5,), (5,), (5,), (), (9,), (), ()):
        scratch.append(dma(shape))
    results = (
        jax.ShapeDtypeStruct((ROWS, D), BF16),
        jax.ShapeDtypeStruct((D, FF), BF16),
        jax.ShapeDtypeStruct((FF, D), BF16),
    )
    held = pl.pallas_call(
        kernel,
        out_shape=tuple(pltpu.VMEM(r.shape, r.dtype) for r in results),
        in_specs=[hbm] * 4,
        out_specs=(vmem, vmem, vmem),
        scratch_shapes=scratch,
        compiler_params=pltpu.CompilerParams(collective_id=0, has_side_effects=True, vmem_limit_bytes=40 * 2**20),
        cost_estimate=pl.CostEstimate(flops=10 * TOK * D * FF, bytes_accessed=8 * D * FF, transcendentals=TOK * HALF // 4),
    )(*(pltpu.with_memory_space_constraint(arg, pltpu.HBM) for arg in (tokens, grad_out, w_in, w_out)))
    return pl.pallas_call(
        write_out,
        out_shape=tuple(pltpu.HBM(r.shape, r.dtype) for r in results),
        in_specs=[vmem] * 3,
        out_specs=(hbm, hbm, hbm),
        scratch_shapes=[dma((5,))],
        compiler_params=pltpu.CompilerParams(vmem_limit_bytes=8 * 2**20),
        cost_estimate=pl.CostEstimate(flops=0, bytes_accessed=8 * D * FF, transcendentals=0),
    )(*(pltpu.with_memory_space_constraint(array, pltpu.VMEM) for array in held))


def solution(mesh):
    return jax.shard_map(
        per_device,
        mesh=mesh,
        in_specs=(P("col", "row"), P("col", "row"), P("row", "col"), P("col", "row")),
        out_specs=(P("col", "row"), P("row", "col"), P("col", "row")),
        check_vma=False,
    )
```

time: 78.1 us -> 64.5 us (0.83)
  Pallas kernels: 73.9 us -> 63.8 us
  local copies, waits for them, and re-layouts: 3.43 us -> 0 us
    pallas_call x1, Pallas kernels: 69.3 us -> 61.5 us  [per_device(): pl.pallas_call(kernel, out_shape=tuple((pltpu.VMEM(r.shape, r.dtype) for...]
    unnamed x6 -> x0, local copies, waits for them, and re-layouts: 3.43 us -> none
    pallas_call x1, Pallas kernels: 4.63 us -> 2.24 us  [per_device(): pl.pallas_call(write_out, out_shape=tuple((pltpu.HBM(r.shape, r.dtype) fo...]
where the time goes in v2:
time: 64.5 us; the launch traced here: 64.4 us
  Pallas kernels  63.8 us (99%)
    pallas_call x1, Pallas kernels, per_device(): pl.pallas_call(kernel, out_shape=tuple((pltpu.VMEM(r.shape, r.dtype) for...  61.5 us
    pallas_call x1, Pallas kernels, per_device(): pl.pallas_call(write_out, out_shape=tuple((pltpu.HBM(r.shape, r.dtype) fo...  2.24 us

profile of v2, /device:TPU:1, one launch (start us, length us, event | category | flops | bytes accessed | tf_op | source)
XLA Modules:
  0.0 64.4 jit_solution(9804632930372451237)
XLA Ops:
  0.6 61.5 %shard_map.67 = (bf16[16,1536]{1,0:T(8,128)(2,1)S(1)}, bf16[1536,768]{1,0:T(8,128)(2,1)S(1)}, bf16[768,1536]{1,0:T(8,128)(2,1)S(1)}) custom-call(bf16[16,1536]{1,0:T(8,128)(2,1)} %tok_hbm.1, bf16[16,1536]{1,0:T(8,128)(2,1)} %grad_hbm.1, bf16[1536,768]{1,0:T(8,128)(2,1)} %win_hbm.1, bf16[768,1536]{1,0:T(8,128)(2,1)} %wout_hbm.1), custom_call_target="tpu_custom_call" | custom-call | flops 6039797760 | bytes 9437184 | tf_op jit(solution)/shard_map/pallas_call | solution.py:378
  62.2 2.2 %shard_map.68 = (bf16[16,1536]{1,0:T(8,128)(2,1)}, bf16[1536,768]{1,0:T(8,128)(2,1)}, bf16[768,1536]{1,0:T(8,128)(2,1)}) custom-call(bf16[16,1536]{1,0:T(8,128)(2,1)S(1)} %get-tuple-element.6.a, bf16[1536,768]{1,0:T(8,128)(2,1)S(1)} %get-tuple-element.7.b, bf16[768,1536]{1,0:T(8,128)(2,1)S(1)} %get-tuple-element.8.c), custom_call_target="tpu_custom_call" | custom-call | bytes 9437184 | tf_op jit(solution)/shard_map/pallas_call | solution.py:387

commit v3 on v2

--- a/solution.py
+++ b/solution.py
@@ -14,27 +14,33 @@
 ROWS = 16
 DIRECT = (4,)
 CA = 640
-ZA = 384
+ZA = 256
 ZB = D - ZA
 GROUPS = ((0, 4), (4, 8), (12, 8), (20, 8), (28, 4))
+MERGE = True
+ZSLOT = {1: 0, 2: 2, 4: 4} if MERGE else {1: 0, 2: 2, 3: 4, 4: 6}
+ZSUMS = 5 if MERGE else 7
 XOFF = (0, 1, -1, 2)
 ORDER = (
-    ("z", 1, 0, 0, 0), ("x", 0, 0, 0), ("T", 2, 0), ("T", 2, 1), ("z", 0, 0, 0, 0), ("T", 2, 2), ("x", 1, 0, 0),
-    ("f", 0, 0, 0, 1), ("f", 0, 0, 0, 2), ("z", 1, 1, 1, 0), ("x", 1, 1, 0), ("z", 1, 1, 0, 0), ("x", 1, 1, 1),
-    ("z", 0, 0, 0, 2), ("T", 1, 1), ("z", 0, 0, 0, 3), ("f", 1, 0, 0, 2), ("z", 0, 0, 0, 1), ("f", 1, 0, 0, 1),
-    ("x", 1, 2, 1), ("x", 1, 2, 0), ("z", 1, 2, 0, 0), ("z", 0, 1, 1, 0), ("z", 0, 1, 0, 0), ("f", 1, 1, 1, 1),
-    ("z", 1, 2, 1, 0), ("z", 0, 1, 0, 3), ("f", 1, 1, 0, 1), ("f", 1, 1, 0, 2), ("T", 1, 0), ("z", 0, 1, 1, 2),
-    ("f", 1, 1, 1, 2), ("P", 0), ("z", 0, 1, 0, 1), ("f", 1, 2, 1, 1), ("f", 1, 2, 1, 2), ("Q", 0), ("x", 1, 3, 0),
-    ("z", 0, 1, 0, 2), ("z", 0, 1, 1, 1), ("z", 1, 3, 0, 0), ("f", 1, 2, 0, 1), ("f", 1, 2, 0, 2), ("x", 1, 3, 1),
-    ("z", 1, 3, 1, 0), ("z", 0, 1, 1, 3), ("z", 0, 2, 1, 0), ("z", 0, 2, 0, 0), ("T", 1, 5), ("S2", 0),
-    ("z", 0, 2, 0, 3), ("P", 1), ("Q", 1), ("f", 1, 3, 0, 1), ("f", 1, 3, 0, 2), ("z", 0, 2, 1, 2), ("z", 0, 2, 0, 1),
-    ("z", 0, 2, 0, 2), ("S2", 1), ("z", 0, 2, 1, 1), ("P", 2), ("z", 0, 2, 1, 3), ("f", 1, 3, 1, 2), ("f", 1, 3, 1, 1),
-    ("Q", 2), ("z", 0, 3, 1, 0), ("S2", 2), ("z", 0, 3, 0, 0), ("x", 1, 4, 0), ("P", 3), ("z", 0, 3, 1, 1),
-    ("z", 0, 3, 0, 2), ("S3", 1), ("Q", 3), ("z", 0, 3, 0, 1), ("z", 0, 3, 1, 2), ("z", 0, 3, 1, 3), ("z", 0, 3, 0, 3),
-    ("T", 1, 2), ("S2", 3), ("T", 1, 4), ("S3", 2), ("P", 4), ("Q", 4), ("S4", 1), ("S2", 4), ("T", 1, 3), ("S3", 3),
-    ("S5", 1), ("S3", 0), ("S4", 2), ("S3", 4), ("S5", 2), ("S4", 3), ("S6", 1, 1), ("S4", 0), ("S6", 1, 0), ("S5", 3),
-    ("S4", 4), ("S5", 4), ("S5", 0), ("S6", 2, 1), ("S6", 2, 0), ("S6", 4, 0), ("S6", 3, 0), ("S6", 3, 1), ("W", 0),
-    ("E1",), ("S6", 0, 0), ("W", 1), ("E3",), ("E2",),
+    ("z", 1, 0, 0, 0), ("x", 0, 0, 0), ("z", 0, 0, 0, 0), ("x", 1, 0, 0), ("f", 0, 0, 0, 1), ("f", 0, 0, 0, 2),
+    ("z", 1, 1, 0, 0), ("z", 1, 1, 1, 0), ("x", 1, 1, 1), ("T", 1, 4), ("x", 1, 1, 0), ("f", 1, 0, 0, 2),
+    ("z", 0, 0, 0, 1), ("T", 1, 2), ("z", 0, 0, 0, 2), ("T", 2, 2), ("f", 1, 0, 0, 1), ("z", 0, 0, 0, 3),
+    ("x", 1, 2, 0), ("T", 1, 1), ("f", 1, 1, 1, 2), ("z", 1, 2, 0, 0), ("z", 0, 1, 0, 0), ("z", 1, 2, 1, 0),
+    ("f", 1, 1, 1, 1), ("z", 0, 1, 1, 0), ("T", 2, 1), ("f", 1, 1, 0, 2), ("f", 1, 1, 0, 1), ("z", 0, 1, 1, 2),
+    ("x", 1, 2, 1), ("T", 2, 0), ("z", 0, 1, 0, 1), ("z", 0, 1, 0, 3), ("T", 1, 3), ("z", 0, 1, 0, 2),
+    ("z", 0, 1, 1, 3), ("f", 1, 2, 0, 1), ("f", 1, 2, 0, 2), ("x", 1, 3, 1), ("z", 1, 3, 1, 0), ("z", 0, 1, 1, 1),
+    ("z", 1, 3, 0, 0), ("P", 1), ("Q", 1), ("x", 1, 3, 0), ("f", 1, 2, 1, 1), ("z", 0, 2, 1, 0), ("z", 0, 2, 1, 2),
+    ("f", 1, 2, 1, 2), ("z", 0, 2, 0, 0), ("P", 0), ("z", 0, 2, 0, 1), ("z", 0, 2, 1, 3), ("S2", 1), ("z", 0, 2, 0, 3),
+    ("T", 1, 5), ("z", 0, 2, 0, 2), ("f", 1, 3, 1, 1), ("Q", 0), ("z", 0, 2, 1, 1), ("f", 1, 3, 1, 2),
+    ("f", 1, 3, 0, 2), ("f", 1, 3, 0, 1), ("x", 1, 4, 0), ("S2", 0), ("P", 2), ("Q", 2), ("S3", 1, 0),
+    ("z", 0, 3, 0, 3), ("z", 0, 3, 1, 0), ("z", 0, 3, 0, 0), ("T", 1, 0), ("z", 0, 3, 1, 2), ("z", 0, 3, 0, 1),
+    ("z", 0, 3, 1, 3), ("S3", 1, 1), ("z", 0, 3, 0, 2), ("P", 3), ("Q", 3), ("S2", 2), ("z", 0, 3, 1, 1), ("S2", 3),
+    ("P", 4), ("Q", 4), ("S4", 1, 0), ("S4", 1, 1), ("S3", 2, 0), ("S2", 4), ("S5", 1, 1), ("S3", 3, 0), ("S5", 1, 0),
+    ("S3", 3, 1), ("S3", 2, 1), ("S4", 2, 0), ("S3", 4, 0), ("S5", 2, 0), ("S4", 3, 0), ("S3", 0, 0), ("S4", 3, 1),
+    ("S5", 3, 0), ("S6", 1, 0), ("S5", 3, 1), ("S4", 4, 0), ("S4", 2, 1), ("S6", 1, 1), ("S4", 0, 0), ("S5", 4, 0),
+    ("S5", 2, 1), ("S6", 2, 0), ("S5", 0, 0), ("MA", 1), ("S6", 3, 0), ("MA", 0), ("S6", 3, 1), ("W", 1, 1),
+    ("W", 1, 0), ("S6", 4, 0), ("MZ", 0), ("S6", 2, 1), ("MZ", 1), ("E1",), ("W", 0, 0), ("S6", 0, 0), ("W", 0, 1),
+    ("E3",), ("E2",),
 )
 
 
@@ -63,7 +69,7 @@
 
 def kernel(
     tok_hbm, grad_hbm, win_hbm, wout_hbm, GIN, GW1, GW2,
-    X, W1, W2, W1T, W2T, KS, KO, KR, C, R, H, G, RA, SA, RX, RB, SB, RZ, OUT,
+    X, W1, W2, W1T, W2T, KS, KO, KR, C, R, H, G, RA, RM, SA, RX, RB, SB, HOLD, RZ, RN, OUT,
     local_sem, sent,
     a_recv, b_recv, k_recv, r_recv, y_recv, h_recv, ra_recv, rb_recv, rx_recv, rz_recv,
 ):
@@ -186,56 +192,59 @@
     def q(s):
         product(s, 1)
 
-    def quarter(s, i):
-        first, n = rows(s)
-        return pl.ds(pl.multiple_of(first + i * (n // 4), ROWS), n // 4)
-
-    def sum_copy(s, dy):
-        n = rows(s)[1] // 4
-        there = R.at[dy - 1, :, pl.ds(rows(s)[0] // 4, n)]
-        return remote(C.at[:, quarter(s, lax.rem(y + dy, 4))], there, 3, r_recv.at[s], at(dy=dy))
+    def first(s, d):
+        return ROWS * block(s, d, 0)
+
+    def quarter(s, d, i):
+        return pl.ds(pl.multiple_of(first(s, d) + i * ROWS, ROWS), ROWS)
+
+    def sum_copy(s, d, dy):
+        there = R.at[dy - 1, :, pl.ds(first(s, d) // 4, ROWS)]
+        return remote(C.at[:, quarter(s, d, lax.rem(y + dy, 4))], there, 3, r_recv.at[2 * s + d], at(dy=dy))
 
     def s2(s):
-        first, n = rows(s)
-        part = pl.ds(first, n)
+        part = pl.ds(*rows(s))
         swap_copy(s, 0).wait_recv()
         swap_copy(s, 1).wait_recv()
         C[:, part, :] = (KO[:, part, :] + KR[:, part, :].astype(F32)).astype(BF16)
-        for dy in (2, 1, 3):
-            sum_copy(s, dy).start()
-
-    def part_copy(s, dy):
-        where = H.at[:, quarter(s, y), pl.ds(0, HALF)]
-        return remote(where, where, 4, y_recv.at[s], at(dy=dy))
-
-    def s3(s):
-        part = pl.ds(rows(s)[0] // 4, rows(s)[1] // 4)
+        for d in ways(s):
+            for dy in (2, 1, 3):
+                sum_copy(s, d, dy).start()
+
+    def part_copy(s, d, dy):
+        where = H.at[:, quarter(s, d, y), pl.ds(0, HALF)]
+        return remote(where, where, 4, y_recv.at[2 * s + d], at(dy=dy))
+
+    def s3(s, d):
+        part = pl.ds(first(s, d) // 4, ROWS)
         landed = R.at[:, :, part]
-        remote(landed, landed, 3, r_recv.at[s], at(dy=1)).wait_recv()
-        total = C[:, quarter(s, y), :].astype(F32)
+        remote(landed, landed, 3, r_recv.at[2 * s + d], at(dy=1)).wait_recv()
+        total = C[:, quarter(s, d, y), :].astype(F32)
         for i in range(3):
             total += R[i, :, part, :].astype(F32)
         activated, grad_pre = gelu_pair(total[0], total[1])
-        H[0, quarter(s, y), 0:HALF] = activated
-        H[1, quarter(s, y), 0:HALF] = grad_pre
+        H[0, quarter(s, d, y), 0:HALF] = activated
+        H[1, quarter(s, d, y), 0:HALF] = grad_pre
         for dy in (2, 1, 3):
-            part_copy(s, dy).start()
-
-    def half_copy(s):
-        first, n = rows(s)
-        part = pl.ds(first, n)
-        return remote(H.at[:, part, pl.ds(0, HALF)], H.at[:, part, pl.ds(HALF, HALF)], 5, h_recv.at[s], at(other=True))
-
-    def s4(s):
-        first, n = rows(s)
-        landed = H.at[:, pl.ds(first, 3 * n // 4), pl.ds(0, HALF)]
-        remote(landed, landed, 4, y_recv.at[s], at(dy=1)).wait_recv()
-        half_copy(s).start()
+            part_copy(s, d, dy).start()
+
+    def half_copy(s, d):
+        part = pl.ds(first(s, d), 4 * ROWS)
+        there = H.at[:, part, pl.ds(HALF, HALF)]
+        return remote(H.at[:, part, pl.ds(0, HALF)], there, 5, h_recv.at[2 * s + d], at(other=True))
+
+    def s4(s, d):
+        landed = H.at[:, pl.ds(first(s, d), 3 * ROWS), pl.ds(0, HALF)]
+        remote(landed, landed, 4, y_recv.at[2 * s + d], at(dy=1)).wait_recv()
+        half_copy(s, d).start()
+
+    def z_copy(src, s, d, kind, recv, straight, added):
+        if MERGE and s == 3:
+            return remote(src, added.at[d], kind, recv.at[1 + d], at(dz=1 if d else -1))
+        return remote(src, straight.at[ZSLOT[s] + d], kind, recv.at[0], at(dz=s if d else -s))
 
     def ra_copy(s, d):
-        i = 2 * (s - 1) + d
-        src = G.at[pl.ds(ROWS * block(s, d, 0), 4 * ROWS), pl.ds(0, ZA)]
-        return remote(src, RA.at[i], 6, ra_recv, at(dz=s if d else -s))
+        return z_copy(G.at[pl.ds(first(s, d), 4 * ROWS), pl.ds(0, ZA)], s, d, 6, ra_recv, RA, RM)
 
     def rb_copy(s, d, f):
         i = 2 * s + d
@@ -243,50 +252,60 @@
         return remote(src, RB.at[i, f - 1], 7, rb_recv.at[i], at(dx=XOFF[f]))
 
     def rz_copy(s, d):
-        i = 2 * (s - 1) + d
-        return remote(SB.at[i], RZ.at[i], 8, rz_recv, at(dz=s if d else -s))
+        return z_copy(SB.at[2 * (s - 1) + d], s, d, 8, rz_recv, RZ, RN)
 
     def rx_copy(f):
         src = SA.at[pl.ds(ROWS * f, ROWS)]
         return remote(src, RX.at[f - 1], 9, rx_recv, at(dx=XOFF[f]))
 
-    def s5(s):
-        half_copy(s).wait_recv()
-        first, n = rows(s)
-        part = pl.ds(first, n)
+    def s5(s, d):
+        half_copy(s, d).wait_recv()
+        part = pl.ds(first(s, d), 4 * ROWS)
         G[part, :] = dot(H[1, part, :], W1T[...], (1, 0)).astype(BF16)
-        for d in ways(s):
-            for f in (3, 1, 2):
-                rb_copy(s, d, f).start()
-            if s:
-                ra_copy(s, d).start()
+        for f in (3, 1, 2):
+            rb_copy(s, d, f).start()
+        if s and not (MERGE and s == 2):
+            ra_copy(s, d).start()
+
+    def ma(d):
+        remote(RM.at[d], RM.at[d], 6, ra_recv.at[1 + d], at(dz=1)).wait_recv()
+        part = pl.ds(first(2, d), 4 * ROWS)
+        G[part, pl.ds(0, ZA)] = (G[part, pl.ds(0, ZA)].astype(F32) + RM[d].astype(F32)).astype(BF16)
+        ra_copy(2, d).start()
 
     def s6(s, d):
         i = 2 * s + d
         remote(RB.at[i], RB.at[i], 7, rb_recv.at[i], at(dx=1)).wait_recv()
-        total = G[pl.ds(ROWS * block(s, d, 0), ROWS), pl.ds(ZA, ZB)].astype(F32)
+        total = G[pl.ds(first(s, d), ROWS), pl.ds(ZA, ZB)].astype(F32)
         for j in range(3):
             total += RB[i, j].astype(F32)
-        if s:
+        if s == 0:
+            OUT[:, pl.ds(ZA, ZB)] = total
+        elif MERGE and s == 2:
+            HOLD[d] = total
+        else:
             SB[2 * (s - 1) + d] = total.astype(BF16)
             rz_copy(s, d).start()
+
+    def mz(d):
+        remote(RN.at[d], RN.at[d], 8, rz_recv.at[1 + d], at(dz=1)).wait_recv()
+        SB[2 + d] = (HOLD[d] + RN[d].astype(F32)).astype(BF16)
+        rz_copy(2, d).start()
+
+    def w(i, j):
+        if i == 0:
+            part = pl.ds(j * (D // 2), D // 2)
+            total = dot(X[0, :, part], H[1], (0, 0)).astype(BF16)
+            GW1[part, pl.ds(mine, HALF)] = total[:, :HALF]
+            GW1[part, pl.ds(theirs, HALF)] = total[:, HALF:]
         else:
-            OUT[:, pl.ds(ZA, ZB)] = total
-
-    def w(i):
-        if i == 0:
-            total = dot(X[0], H[1], (0, 0)).astype(BF16)
-            GW1[:, pl.ds(mine, HALF)] = total[:, :HALF]
-            GW1[:, pl.ds(theirs, HALF)] = total[:, HALF:]
-        else:
-            total = dot(H[0], X[1], (0, 0)).astype(BF16)
-            GW2[pl.ds(mine, HALF), :] = total[:HALF]
-            GW2[pl.ds(theirs, HALF), :] = total[HALF:]
+            total = dot(H[0, :, pl.ds(j * HALF, HALF)], X[1], (0, 0)).astype(BF16)
+            GW2[pl.ds(theirs if j else mine, HALF), :] = total
 
     def e1():
-        remote(RA, RA, 6, ra_recv, at(dz=1)).wait_recv()
+        remote(RA, RA, 6, ra_recv.at[0], at(dz=1)).wait_recv()
         total = G[pl.ds(0, 4 * ROWS), pl.ds(0, ZA)].astype(F32)
-        for i in range(7):
+        for i in range(ZSUMS):
             total += RA[i].astype(F32)
         OUT[:, pl.ds(0, ZA)] = total[:ROWS]
         SA[...] = total.astype(BF16)
@@ -294,9 +313,9 @@
             rx_copy(f).start()
 
     def e2():
-        remote(RZ, RZ, 8, rz_recv, at(dz=1)).wait_recv()
+        remote(RZ, RZ, 8, rz_recv.at[0], at(dz=1)).wait_recv()
         total = OUT[:, pl.ds(ZA, ZB)]
-        for i in range(7):
+        for i in range(ZSUMS):
             total += RZ[i].astype(F32)
         GIN[:, pl.ds(ZA, ZB)] = total.astype(BF16)
 
@@ -309,7 +328,7 @@
 
     steps = {
         "z": along_z, "x": along_x, "f": further_x, "T": turn, "P": p, "Q": q, "S2": s2, "S3": s3, "S4": s4, "S5": s5,
-        "S6": s6, "W": w, "E1": e1, "E2": e2, "E3": e3,
+        "S6": s6, "MA": ma, "MZ": mz, "W": w, "E1": e1, "E2": e2, "E3": e3,
     }
     for name, *args in ORDER:
         steps[name](*args)
@@ -321,7 +340,7 @@
         C.at[:, pl.ds(0, 3 * TOK // 4)],
         H.at[:, pl.ds(0, 3 * TOK // 4), pl.ds(0, HALF)],
         H.at[:, :, pl.ds(0, HALF)],
-        RA,
+        G.at[pl.ds(0, 28 * ROWS), pl.ds(0, ZA)],
         G.at[pl.ds(0, 24 * ROWS), pl.ds(ZA, ZB)],
         SB,
         RX,
@@ -358,17 +377,20 @@
         pltpu.VMEM((3, 2, TOK // 4, HALF), BF16),
         pltpu.VMEM((2, TOK, FF), BF16),
         pltpu.VMEM((TOK, D), BF16),
-        pltpu.VMEM((7, 4 * ROWS, ZA), BF16),
+        pltpu.VMEM((ZSUMS, 4 * ROWS, ZA), BF16),
+        pltpu.VMEM((2, 4 * ROWS, ZA), BF16),
         pltpu.VMEM((4 * ROWS, ZA), BF16),
         pltpu.VMEM((3, ROWS, ZA), BF16),
         pltpu.VMEM((9, 3, ROWS, ZB), BF16),
         pltpu.VMEM((7, ROWS, ZB), BF16),
-        pltpu.VMEM((7, ROWS, ZB), BF16),
+        pltpu.VMEM((2, ROWS, ZB), F32),
+        pltpu.VMEM((ZSUMS, ROWS, ZB), BF16),
+        pltpu.VMEM((2, ROWS, ZB), BF16),
         pltpu.VMEM((ROWS, D), F32),
         dma((6,)),
         dma((10,)),
     ]
-    for shape in ((32,), (32,), (5, 2), (5,), (5,), (5,), (), (9,), (), ()):
+    for shape in ((32,), (32,), (5, 2), (9,), (9,), (9,), (3,), (9,), (), (3,)):
         scratch.append(dma(shape))
     results = (
         jax.ShapeDtypeStruct((ROWS, D), BF16),

time: 64.5 us -> 63.3 us (0.981)
  Pallas kernels: 63.8 us -> 62.6 us
    pallas_call x1, Pallas kernels: 61.5 us -> 60.4 us  [per_device(): pl.pallas_call(kernel, out_shape=tuple((pltpu.VMEM(r.shape, r.dtype) for...]
where the time goes in v3:
time: 63.3 us
  Pallas kernels  62.6 us (99%)
  between operations  0.64 us (1%)
    pallas_call x1, Pallas kernels, per_device(): pl.pallas_call(kernel, out_shape=tuple((pltpu.VMEM(r.shape, r.dtype) for...  60.4 us
    pallas_call x1, Pallas kernels, per_device(): pl.pallas_call(write_out, out_shape=tuple((pltpu.HBM(r.shape, r.dtype) fo...  2.24 us

profile of v3, /device:TPU:1, one launch (start us, length us, event | category | flops | bytes accessed | tf_op | source)
XLA Modules:
  0.0 63.3 jit_solution(8982635253972839587)
XLA Ops:
  0.6 60.4 %shard_map.67 = (bf16[16,1536]{1,0:T(8,128)(2,1)S(1)}, bf16[1536,768]{1,0:T(8,128)(2,1)S(1)}, bf16[768,1536]{1,0:T(8,128)(2,1)S(1)}) custom-call(bf16[16,1536]{1,0:T(8,128)(2,1)} %tok_hbm.1, bf16[16,1536]{1,0:T(8,128)(2,1)} %grad_hbm.1, bf16[1536,768]{1,0:T(8,128)(2,1)} %win_hbm.1, bf16[768,1536]{1,0:T(8,128)(2,1)} %wout_hbm.1), custom_call_target="tpu_custom_call" | custom-call | flops 6039797760 | bytes 9437184 | tf_op jit(solution)/shard_map/pallas_call | solution.py:400
  61.0 2.2 %shard_map.68 = (bf16[16,1536]{1,0:T(8,128)(2,1)}, bf16[1536,768]{1,0:T(8,128)(2,1)}, bf16[768,1536]{1,0:T(8,128)(2,1)}) custom-call(bf16[16,1536]{1,0:T(8,128)(2,1)S(1)} %get-tuple-element.6.a, bf16[1536,768]{1,0:T(8,128)(2,1)S(1)} %get-tuple-element.7.b, bf16[768,1536]{1,0:T(8,128)(2,1)S(1)} %get-tuple-element.8.c), custom_call_target="tpu_custom_call" | custom-call | bytes 9437184 | tf_op jit(solution)/shard_map/pallas_call | solution.py:409

commit v4 on v3

--- a/solution.py
+++ b/solution.py
@@ -17,30 +17,29 @@
 ZA = 256
 ZB = D - ZA
 GROUPS = ((0, 4), (4, 8), (12, 8), (20, 8), (28, 4))
-MERGE = True
+MERGE = False
 ZSLOT = {1: 0, 2: 2, 4: 4} if MERGE else {1: 0, 2: 2, 3: 4, 4: 6}
 ZSUMS = 5 if MERGE else 7
 XOFF = (0, 1, -1, 2)
 ORDER = (
-    ("z", 1, 0, 0, 0), ("x", 0, 0, 0), ("z", 0, 0, 0, 0), ("x", 1, 0, 0), ("f", 0, 0, 0, 1), ("f", 0, 0, 0, 2),
-    ("z", 1, 1, 0, 0), ("z", 1, 1, 1, 0), ("x", 1, 1, 1), ("T", 1, 4), ("x", 1, 1, 0), ("f", 1, 0, 0, 2),
-    ("z", 0, 0, 0, 1), ("T", 1, 2), ("z", 0, 0, 0, 2), ("T", 2, 2), ("f", 1, 0, 0, 1), ("z", 0, 0, 0, 3),
-    ("x", 1, 2, 0), ("T", 1, 1), ("f", 1, 1, 1, 2), ("z", 1, 2, 0, 0), ("z", 0, 1, 0, 0), ("z", 1, 2, 1, 0),
-    ("f", 1, 1, 1, 1), ("z", 0, 1, 1, 0), ("T", 2, 1), ("f", 1, 1, 0, 2), ("f", 1, 1, 0, 1), ("z", 0, 1, 1, 2),
-    ("x", 1, 2, 1), ("T", 2, 0), ("z", 0, 1, 0, 1), ("z", 0, 1, 0, 3), ("T", 1, 3), ("z", 0, 1, 0, 2),
-    ("z", 0, 1, 1, 3), ("f", 1, 2, 0, 1), ("f", 1, 2, 0, 2), ("x", 1, 3, 1), ("z", 1, 3, 1, 0), ("z", 0, 1, 1, 1),
-    ("z", 1, 3, 0, 0), ("P", 1), ("Q", 1), ("x", 1, 3, 0), ("f", 1, 2, 1, 1), ("z", 0, 2, 1, 0), ("z", 0, 2, 1, 2),
-    ("f", 1, 2, 1, 2), ("z", 0, 2, 0, 0), ("P", 0), ("z", 0, 2, 0, 1), ("z", 0, 2, 1, 3), ("S2", 1), ("z", 0, 2, 0, 3),
-    ("T", 1, 5), ("z", 0, 2, 0, 2), ("f", 1, 3, 1, 1), ("Q", 0), ("z", 0, 2, 1, 1), ("f", 1, 3, 1, 2),
-    ("f", 1, 3, 0, 2), ("f", 1, 3, 0, 1), ("x", 1, 4, 0), ("S2", 0), ("P", 2), ("Q", 2), ("S3", 1, 0),
-    ("z", 0, 3, 0, 3), ("z", 0, 3, 1, 0), ("z", 0, 3, 0, 0), ("T", 1, 0), ("z", 0, 3, 1, 2), ("z", 0, 3, 0, 1),
-    ("z", 0, 3, 1, 3), ("S3", 1, 1), ("z", 0, 3, 0, 2), ("P", 3), ("Q", 3), ("S2", 2), ("z", 0, 3, 1, 1), ("S2", 3),
-    ("P", 4), ("Q", 4), ("S4", 1, 0), ("S4", 1, 1), ("S3", 2, 0), ("S2", 4), ("S5", 1, 1), ("S3", 3, 0), ("S5", 1, 0),
-    ("S3", 3, 1), ("S3", 2, 1), ("S4", 2, 0), ("S3", 4, 0), ("S5", 2, 0), ("S4", 3, 0), ("S3", 0, 0), ("S4", 3, 1),
-    ("S5", 3, 0), ("S6", 1, 0), ("S5", 3, 1), ("S4", 4, 0), ("S4", 2, 1), ("S6", 1, 1), ("S4", 0, 0), ("S5", 4, 0),
-    ("S5", 2, 1), ("S6", 2, 0), ("S5", 0, 0), ("MA", 1), ("S6", 3, 0), ("MA", 0), ("S6", 3, 1), ("W", 1, 1),
-    ("W", 1, 0), ("S6", 4, 0), ("MZ", 0), ("S6", 2, 1), ("MZ", 1), ("E1",), ("W", 0, 0), ("S6", 0, 0), ("W", 0, 1),
-    ("E3",), ("E2",),
+    ("z", 1, 0, 0, 0), ("x", 0, 0, 0), ("T", 1, 5), ("z", 0, 0, 0, 0), ("x", 1, 0, 0), ("T", 1, 1), ("z", 1, 1, 0, 0),
+    ("f", 0, 0, 0, 2), ("f", 0, 0, 0, 1), ("z", 1, 1, 1, 0), ("x", 1, 1, 1), ("z", 0, 0, 0, 1), ("x", 1, 1, 0),
+    ("T", 1, 2), ("T", 1, 0), ("T", 2, 1), ("f", 1, 0, 0, 2), ("T", 1, 3), ("z", 0, 0, 0, 2), ("f", 1, 0, 0, 1),
+    ("z", 0, 1, 1, 0), ("z", 0, 1, 0, 0), ("x", 1, 2, 0), ("T", 1, 4), ("z", 0, 0, 0, 3), ("x", 1, 2, 1),
+    ("z", 0, 1, 0, 1), ("f", 1, 1, 1, 1), ("z", 0, 1, 1, 1), ("f", 1, 1, 1, 2), ("z", 1, 2, 0, 0), ("T", 2, 0),
+    ("f", 1, 1, 0, 1), ("z", 1, 2, 1, 0), ("f", 1, 1, 0, 2), ("z", 0, 1, 0, 2), ("T", 2, 2), ("z", 0, 1, 1, 2),
+    ("P", 0), ("Q", 0), ("f", 1, 2, 0, 1), ("z", 0, 1, 0, 3), ("z", 0, 1, 1, 3), ("f", 1, 2, 0, 2), ("z", 0, 2, 1, 0),
+    ("f", 1, 2, 1, 2), ("f", 1, 2, 1, 1), ("z", 0, 2, 0, 0), ("S2", 0), ("x", 1, 3, 1), ("x", 1, 3, 0),
+    ("z", 1, 3, 0, 0), ("z", 0, 2, 0, 1), ("z", 1, 3, 1, 0), ("P", 1), ("Q", 1), ("z", 0, 2, 0, 3), ("z", 0, 2, 1, 2),
+    ("z", 0, 2, 1, 1), ("z", 0, 2, 0, 2), ("P", 2), ("S2", 1), ("Q", 2), ("z", 0, 3, 0, 0), ("z", 0, 2, 1, 3),
+    ("x", 1, 4, 0), ("S2", 2), ("z", 0, 3, 1, 0), ("z", 0, 3, 0, 1), ("z", 0, 3, 1, 2), ("z", 0, 3, 1, 1),
+    ("f", 1, 3, 1, 2), ("z", 0, 3, 0, 3), ("z", 0, 3, 0, 2), ("f", 1, 3, 1, 1), ("f", 1, 3, 0, 2), ("z", 0, 3, 1, 3),
+    ("f", 1, 3, 0, 1), ("S3", 1, 0), ("S3", 1, 1), ("S3", 2, 0), ("P", 4), ("Q", 4), ("P", 3), ("Q", 3), ("S4", 1, 0),
+    ("S3", 2, 1), ("S4", 1, 1), ("S2", 3), ("S5", 1, 0), ("S4", 2, 0), ("S3", 4, 0), ("S5", 1, 1), ("S5", 2, 0),
+    ("S4", 2, 1), ("S3", 3, 0), ("S3", 3, 1), ("S5", 2, 1), ("S3", 0, 0), ("S6", 1, 0), ("S5", 4, 0), ("S4", 3, 0),
+    ("S6", 1, 1), ("S4", 3, 1), ("S5", 3, 0), ("S4", 0, 0), ("S6", 2, 1), ("S6", 2, 0), ("S5", 3, 1), ("S5", 0, 0),
+    ("W", 1, 0), ("S6", 4, 0), ("W", 0, 0), ("W", 1, 1), ("S6", 3, 0), ("S6", 3, 1), ("W", 0, 1), ("E1",),
+    ("S6", 0, 0), ("E3",), ("E2",),
 )
 
 
@@ -69,9 +68,9 @@
 
 def kernel(
     tok_hbm, grad_hbm, win_hbm, wout_hbm, GIN, GW1, GW2,
-    X, W1, W2, W1T, W2T, KS, KO, KR, C, R, H, G, RA, RM, SA, RX, RB, SB, HOLD, RZ, RN, OUT,
+    X, W1, W2, W1T, W2T, KS, KO, KR, C, R, R8, H, G, RA, RM, SA, RX, RB, SB, HOLD, RZ, RN, OUT,
     local_sem, sent,
-    a_recv, b_recv, k_recv, r_recv, y_recv, h_recv, ra_recv, rb_recv, rx_recv, rz_recv,
+    a_recv, b_recv, k_recv, r_recv, r8_recv, y_recv, h_recv, ra_recv, rb_recv, rx_recv, rz_recv,
 ):
     row, col = lax.axis_index("row"), lax.axis_index("col")
     y, core, z, x = row // 2, row % 2, col // 4, col % 4
@@ -96,7 +95,7 @@
         copy.start()
 
     partners = [at(dz=i) for i in range(1, 8)] + [at(dx=i) for i in range(1, 4)] + [at(dy=i) for i in range(1, 4)]
-    partners.append(at(other=True))
+    partners += [at(dy=i, other=True) for i in range(4)]
     barrier = pltpu.get_barrier_semaphore()
     for partner in partners:
         pl.semaphore_signal(barrier, inc=1, device_id=partner, device_id_type=MESH)
@@ -177,9 +176,12 @@
         first, n = rows(s)
         part = pl.ds(first, n)
         total = dot(X[i, part, :], (W1, W2T)[i][...], (1, 0))
-        KO[i, part, :] = total[:, :HALF]
         KS[i, part, :] = total[:, HALF:].astype(BF16)
-        swap_copy(s, i).start()
+        if s == 4:
+            C[i, part, :] = total[:, :HALF].astype(BF16)
+        else:
+            KO[i, part, :] = total[:, :HALF]
+            swap_copy(s, i).start()
 
     def p(s):
         for d in ways(s):
@@ -191,6 +193,12 @@
 
     def q(s):
         product(s, 1)
+        if s == 4:
+            cross_sum(2).start()
+            for dy in (2, 1, 3):
+                sum_copy(s, 0, dy).start()
+            for dy in (1, 3, 0):
+                cross_sum(dy).start()
 
     def first(s, d):
         return ROWS * block(s, d, 0)
@@ -201,6 +209,15 @@
     def sum_copy(s, d, dy):
         there = R.at[dy - 1, :, pl.ds(first(s, d) // 4, ROWS)]
         return remote(C.at[:, quarter(s, d, lax.rem(y + dy, 4))], there, 3, r_recv.at[2 * s + d], at(dy=dy))
+
+    def cross_sum(dy):
+        src = KS.at[:, quarter(4, 0, lax.rem(y + dy, 4))]
+        return remote(src, R8.at[dy], 2, r8_recv, at(dy=dy, other=True))
+
+    def cross_part(dy):
+        where = quarter(4, 0, y)
+        there = H.at[:, where, pl.ds(HALF, HALF)]
+        return remote(H.at[:, where, pl.ds(0, HALF)], there, 5, h_recv.at[8], at(dy=dy, other=True))
 
     def s2(s):
         part = pl.ds(*rows(s))
@@ -222,20 +239,32 @@
         total = C[:, quarter(s, d, y), :].astype(F32)
         for i in range(3):
             total += R[i, :, part, :].astype(F32)
+        if s == 4:
+            remote(R8, R8, 2, r8_recv, at(other=True)).wait_recv()
+            for i in range(4):
+                total += R8[i].astype(F32)
         activated, grad_pre = gelu_pair(total[0], total[1])
         H[0, quarter(s, d, y), 0:HALF] = activated
         H[1, quarter(s, d, y), 0:HALF] = grad_pre
+        if s == 4:
+            cross_part(2).start()
         for dy in (2, 1, 3):
             part_copy(s, d, dy).start()
+        if s == 4:
+            for dy in (1, 3, 0):
+                cross_part(dy).start()
 
     def half_copy(s, d):
         part = pl.ds(first(s, d), 4 * ROWS)
         there = H.at[:, part, pl.ds(HALF, HALF)]
         return remote(H.at[:, part, pl.ds(0, HALF)], there, 5, h_recv.at[2 * s + d], at(other=True))
 
-    def s4(s, d):
+    def quarters(s, d):
         landed = H.at[:, pl.ds(first(s, d), 3 * ROWS), pl.ds(0, HALF)]
         remote(landed, landed, 4, y_recv.at[2 * s + d], at(dy=1)).wait_recv()
+
+    def s4(s, d):
+        quarters(s, d)
         half_copy(s, d).start()
 
     def z_copy(src, s, d, kind, recv, straight, added):
@@ -259,6 +288,8 @@
         return remote(src, RX.at[f - 1], 9, rx_recv, at(dx=XOFF[f]))
 
     def s5(s, d):
+        if s == 4:
+            quarters(s, d)
         half_copy(s, d).wait_recv()
         part = pl.ds(first(s, d), 4 * ROWS)
         G[part, :] = dot(H[1, part, :], W1T[...], (1, 0)).astype(BF16)
@@ -375,6 +406,7 @@
         pltpu.VMEM((2, TOK, HALF), BF16),
         pltpu.VMEM((2, TOK, HALF), BF16),
         pltpu.VMEM((3, 2, TOK // 4, HALF), BF16),
+        pltpu.VMEM((4, 2, ROWS, HALF), BF16),
         pltpu.VMEM((2, TOK, FF), BF16),
         pltpu.VMEM((TOK, D), BF16),
         pltpu.VMEM((ZSUMS, 4 * ROWS, ZA), BF16),
@@ -390,7 +422,7 @@
         dma((6,)),
         dma((10,)),
     ]
-    for shape in ((32,), (32,), (5, 2), (9,), (9,), (9,), (3,), (9,), (), (3,)):
+    for shape in ((32,), (32,), (5, 2), (9,), (), (9,), (9,), (3,), (9,), (), (3,)):
         scratch.append(dma(shape))
     results = (
         jax.ShapeDtypeStruct((ROWS, D), BF16),

time: 63.3 us -> 62.5 us (0.987); the launches traced: 63.3 us -> 61.5 us
  Pallas kernels: 62.6 us -> 60.8 us
    pallas_call x1, Pallas kernels: 60.4 us -> 58.6 us  [per_device(): pl.pallas_call(kernel, out_shape=tuple((pltpu.VMEM(r.shape, r.dtype) for...]
where the time goes in v4:
time: 62.5 us; the launch traced here: 61.5 us
  Pallas kernels  60.8 us (97%)
  between operations  0.64 us (1%)
    pallas_call x1, Pallas kernels, per_device(): pl.pallas_call(kernel, out_shape=tuple((pltpu.VMEM(r.shape, r.dtype) for...  58.6 us
    pallas_call x1, Pallas kernels, per_device(): pl.pallas_call(write_out, out_shape=tuple((pltpu.HBM(r.shape, r.dtype) fo...  2.24 us

profile of v4, /device:TPU:1, one launch (start us, length us, event | category | flops | bytes accessed | tf_op | source)
XLA Modules:
  0.0 61.5 jit_solution(2397492752076860257)
XLA Ops:
  0.6 58.6 %shard_map.67 = (bf16[16,1536]{1,0:T(8,128)(2,1)S(1)}, bf16[1536,768]{1,0:T(8,128)(2,1)S(1)}, bf16[768,1536]{1,0:T(8,128)(2,1)S(1)}) custom-call(bf16[16,1536]{1,0:T(8,128)(2,1)} %tok_hbm.1, bf16[16,1536]{1,0:T(8,128)(2,1)} %grad_hbm.1, bf16[1536,768]{1,0:T(8,128)(2,1)} %win_hbm.1, bf16[768,1536]{1,0:T(8,128)(2,1)} %wout_hbm.1), custom_call_target="tpu_custom_call" | custom-call | flops 6039797760 | bytes 9437184 | tf_op jit(solution)/shard_map/pallas_call | solution.py:432
  59.2 2.2 %shard_map.68 = (bf16[16,1536]{1,0:T(8,128)(2,1)}, bf16[1536,768]{1,0:T(8,128)(2,1)}, bf16[768,1536]{1,0:T(8,128)(2,1)}) custom-call(bf16[16,1536]{1,0:T(8,128)(2,1)S(1)} %get-tuple-element.6.a, bf16[1536,768]{1,0:T(8,128)(2,1)S(1)} %get-tuple-element.7.b, bf16[768,1536]{1,0:T(8,128)(2,1)S(1)} %get-tuple-element.8.c), custom_call_target="tpu_custom_call" | custom-call | bytes 9437184 | tf_op jit(solution)/shard_map/pallas_call | solution.py:441
